TPU v7x, 256 devices: a whole 4x4x8 slice. The times are simulated.
256 devices in a mesh: blk: 16 (over x, y_lo, core), wide: 16 (over y_hi, z).
Axes of the slice: x: 4, y: 4 (y_hi: 2, y_lo: 2; y = y_hi * 2 + y_lo), z: 8, core: 2. Of those that a mesh axis runs over, the one named last changes fastest.
Arguments:
- points: bfloat16 [65536, 32], P(('blk', 'wide')), may hold values from -6 to 6
- inv_length: float32 [32], replicated, may hold values from 0.2 to 0.7
- noise_var: float32 [], replicated, may hold values from 0.1 to 1
- solution: float32 [65536, 128], P(('blk', 'wide')), may hold values from -6 to 6
- residual: float32 [65536, 128], P(('blk', 'wide')), may hold values from -6 to 6
- direction: float32 [65536, 128], P(('blk', 'wide')), may hold values from -6 to 6
Outputs:
- new_solution: float32 [65536, 128], P(('blk', 'wide'))
- new_residual: float32 [65536, 128], P(('blk', 'wide'))
- new_direction: float32 [65536, 128], P(('blk', 'wide'))
All inputs are finite; a program needn't handle non-finite values.
Results may differ from a plain program's by a relative error of at most 0.01.
Values may be sent and summed in bfloat16 or wider, within the bound.
No kernel may reach another device: no remote copies, remote signals or barrier semaphores. Data moves between devices by JAX's collectives and lax.ppermute only.
A program may use at most 64 MiB of HBM per device.

v0:
```python
import functools
import jax
import jax.numpy as jnp
from jax import lax
from jax.sharding import Mesh
from jax.sharding import PartitionSpec as P

WIDE = ("wide_0", "wide_1")
BLK = ("blk_0", "blk_1", "blk_2")
BLK_WIDE = ("blk_0", "blk_1", "blk_2", "wide_0", "wide_1")


def shifted(x, axis, by):
    count = lax.axis_size(axis)
    return lax.ppermute(x, axis, [(i, (i + by) % count) for i in range(count)])


def cut_along(x, dim, count):
    before, after = (x.shape[:dim], x.shape[dim + 1 :])
    return jnp.moveaxis(x.reshape(*before, count, -1, *after), dim, 0)


def sent_and_summed(x, axis, dim):
    count = lax.axis_size(axis)
    blocks = lax.all_to_all(cut_along(x, dim, count), axis, 0, 0, tiled=True)
    return jnp.sum(blocks.astype(jnp.float32), axis=0)


def over_axes(x, axes):
    return functools.reduce(lax.psum, axes, x)


def squares_of(values):
    wide_values = values.astype(jnp.float32)
    return jnp.sum(wide_values * wide_values, axis=1)


def kernel_tile(rows_x, rows_sq, cols_x, cols_sq):
    inner_prod = lax.dot_general(
        rows_x, cols_x, (((1,), (1,)), ((), ())), preferred_element_type=jnp.float32
    )
    dist_sq = jnp.maximum(rows_sq[:, None] + cols_sq[None, :] - 2.0 * inner_prod, 0.0)
    radius = jnp.sqrt(5.0 * dist_sq)
    return ((1.0 + radius + radius * radius / 3.0) * jnp.exp(-radius)).astype(jnp.bfloat16)


def on_device(points, inv_length, noise_var, solution, residual, direction):
    scaled = (points.astype(jnp.float32) * inv_length).astype(jnp.bfloat16)
    low_dir = direction.astype(jnp.bfloat16)
    own_sq = squares_of(scaled)
    block_x, block_p = (
        lax.all_gather(scaled, WIDE, axis=0, tiled=True),
        lax.all_gather(low_dir, WIDE, axis=0, tiled=True),
    )
    block_sq = squares_of(block_x)
    cycle_size = lax.axis_size(BLK)
    empty_sums = jnp.zeros(direction.shape, jnp.float32)
    half_cycle = cycle_size // 2
    row_sums = jnp.dot(
        kernel_tile(block_x, block_sq, scaled, own_sq), low_dir, preferred_element_type=jnp.float32
    )

    def paired_turn(counter, carried):
        piece_x, piece_p, piece_sum, row_total = carried
        piece_x, piece_p = shifted((piece_x, piece_p), BLK, 1)
        piece_sum = shifted(piece_sum, BLK, 1)
        kernel_block = kernel_tile(block_x, block_sq, piece_x, squares_of(piece_x))
        row_total = row_total + jnp.dot(kernel_block, piece_p, preferred_element_type=jnp.float32)
        piece_sum = piece_sum + lax.dot_general(
            kernel_block, block_p, (((0,), (0,)), ((), ())), preferred_element_type=jnp.float32
        )
        return (piece_x, piece_p, piece_sum, row_total)

    result = lax.fori_loop(0, half_cycle - 1, paired_turn, (scaled, low_dir, empty_sums, row_sums))
    home_sums = shifted(result[2], BLK, 1 - half_cycle)
    far_x, far_p = shifted((scaled, low_dir), BLK, half_cycle)
    far_block = kernel_tile(block_x, block_sq, far_x, squares_of(far_x))
    row_sums = result[3] + jnp.dot(far_block, far_p, preferred_element_type=jnp.float32)
    own_image = sent_and_summed(row_sums.astype(jnp.bfloat16), WIDE, 0) + home_sums
    kernel_image = own_image + noise_var * direction
    old_norm = over_axes(jnp.sum(residual * residual, axis=0), BLK_WIDE)
    curvature = over_axes(jnp.sum(direction * kernel_image, axis=0), BLK_WIDE)
    step_length = old_norm / curvature
    new_residual = residual - step_length * kernel_image
    new_norm = over_axes(jnp.sum(new_residual * new_residual, axis=0), BLK_WIDE)
    new_solution = solution + step_length * direction
    new_direction = new_residual + new_norm / old_norm * direction
    return (new_solution, new_residual, new_direction)


def solution(mesh):
    finer = Mesh(
        mesh.devices.reshape(4, 2, 2, 2, 8), ("blk_0", "blk_1", "blk_2", "wide_0", "wide_1")
    )
    placed = (P(BLK_WIDE, None), P(), P(), P(BLK_WIDE, None), P(BLK_WIDE, None), P(BLK_WIDE, None))
    return jax.shard_map(
        on_device,
        mesh=finer,
        in_specs=placed,
        out_specs=(P(BLK_WIDE, None), P(BLK_WIDE, None), P(BLK_WIDE, None)),
        check_vma=False,
    )
```

profile of v0, /device:TPU:10, one launch (start us, length us, event | category | flops | bytes accessed | tf_op | source)
XLA Modules:
  0.0 301.9 jit_solution(7086538707987538601)
XLA Ops:
  7.2 1.5 convert_element_type.38
  8.8 2.2 collective-permute-start.4
  11.8 1.3 multiply_reduce_fusion.5
  13.1 1.4 collective-permute-start.3
  14.5 50.2 %all_gather.6 = bf16[4096,32]{1,0:T(8,128)(2,1)S(1)} all-gather(bf16[256,32]{1,0:T(8,128)(2,1)} %get-tuple-element.156), channel_id=1, replica_groups=mesh['blk_0'=4,'blk_1'=2,'blk_2'=2,'wide_0'=2,'wide_1'=8] {'wide_0','wid..., dimensions={0}, use_global_device_ids=true | all-gather | bytes 278528 | tf_op jit(solution)/shard_map/all_gather | solution.py:52
  65.4 3.8 %fusion.5 = f32[4096,128]{1,0:T(8,128)S(1)} fusion(bf16[256,128]{1,0:T(8,128)(2,1)S(1)} %copy-done.4, bf16[4096,32]{1,0:T(8,128)(2,1)S(1)} %all_gather.6, bf16[256,32]{1,0:T(8,128)(2,1)} %get-tuple-element.156, f32[256]{0:T(256)S(1)} %get-tuple-element.103, f32[4096]{0:T(1024)S(1)} %multiply_reduce_fusion.1), kind=kOutput, calls=%fused_computation.18 | convolution fusion | flops 348127232 | bytes 2458624 | tf_op jit(solution)/shard_map/dot_general | solution.py:59
  69.9 22.2 %all-gather.2.cloned.1.call-done = bf16[4096,128]{1,0:T(8,128)(2,1)} async-done(((bf16[256,128]{1,0:T(8,128)(2,1)}), bf16[4096,128]{1,0:T(8,128)(2,1)}) %all-gather.2.cloned.1.call-update) | async-done | bytes 1048592 | tf_op jit(solution)/shard_map/all_gather | solution.py:53
  92.1 79.3 %while.17 = (s32[]{:T(128)}, bf16[256,32]{1,0:T(8,128)(2,1)}, bf16[256,128]{1,0:T(8,128)(2,1)S(1)}, f32[256,128]{1,0:T(8,128)S(1)}, f32[4096,128]{1,0:T(8,128)S(...) while((s32[]{:T(128)}, bf16[256,32]{1,0:T(8,128)(2,1)}, ...), condition=%wide.region_10.0_spmd.clone, body=%wide.region_8.10_spmd.clone.sunk | while | flops 617176832 | bytes 17647876 | solution.py:74
  92.1 2.5 collective-permute-start.2
  94.7 1.3 collective-permute-done
  96.1 3.1 %multiply_convert_fusion.6 = bf16[4096,256]{1,0:T(8,128)(2,1)S(1)} fusion(bf16[4096,32]{1,0:T(8,128)(2,1)S(1)} %get-tuple-element.181, bf16[256,32]{1,0:T(8,128)(2,1)S(1)} %collective-permute-done, f32[256]{0:T(256)S(1)} %multiply_reduce_fusion.8, f32[4096]{0:T(1024)S(1)} %get-tuple-element.180), kind=kOutput, calls=%fused_computation.2.clone.1 | convolution fusion | flops 79691776 | bytes 2393088 | tf_op jit(solution)/shard_map/while/body/eval_jaxpr/dot_general | solution.py:39
  101.1 1.7 convolution_add_fusion.5
  103.0 3.2 %collective-permute-start.2 = (f32[256,128]{1,0:T(8,128)S(1)}, f32[256,128]{1,0:T(8,128)}, u32[]{:S(2)}, u32[]{:S(2)}) collective-permute-start(f32[256,128]{1,0:T(8,128)S(1)} %broadcast_select_fusion.2), channel_id=1, source_target_pairs={{0,16},{16,32},{32,48},{48,64},{64,80},{80,96},{96,112},{112,128},... | collective-permute-start | bytes 393224 | tf_op jit(solution)/shard_map/while/body/eval_jaxpr/ppermute | solution.py:15
  106.8 3.1 %multiply_convert_fusion.6 = bf16[4096,256]{1,0:T(8,128)(2,1)S(1)} fusion(bf16[4096,32]{1,0:T(8,128)(2,1)S(1)} %get-tuple-element.181, bf16[256,32]{1,0:T(8,128)(2,1)S(1)} %collective-permute-done, f32[256]{0:T(256)S(1)} %multiply_reduce_fusion.8, f32[4096]{0:T(1024)S(1)} %get-tuple-element.180), kind=kOutput, calls=%fused_computation.2.clone.1 | convolution fusion | flops 79691776 | bytes 2393088 | tf_op jit(solution)/shard_map/while/body/eval_jaxpr/dot_general | solution.py:39
  111.8 1.7 convolution_add_fusion.5
  114.7 3.2 %collective-permute-start.2 = (f32[256,128]{1,0:T(8,128)S(1)}, f32[256,128]{1,0:T(8,128)}, u32[]{:S(2)}, u32[]{:S(2)}) collective-permute-start(f32[256,128]{1,0:T(8,128)S(1)} %broadcast_select_fusion.2), channel_id=1, source_target_pairs={{0,16},{16,32},{32,48},{48,64},{64,80},{80,96},{96,112},{112,128},... | collective-permute-start | bytes 393224 | tf_op jit(solution)/shard_map/while/body/eval_jaxpr/ppermute | solution.py:15
  118.1 3.1 %multiply_convert_fusion.6 = bf16[4096,256]{1,0:T(8,128)(2,1)S(1)} fusion(bf16[4096,32]{1,0:T(8,128)(2,1)S(1)} %get-tuple-element.181, bf16[256,32]{1,0:T(8,128)(2,1)S(1)} %collective-permute-done, f32[256]{0:T(256)S(1)} %multiply_reduce_fusion.8, f32[4096]{0:T(1024)S(1)} %get-tuple-element.180), kind=kOutput, calls=%fused_computation.2.clone.1 | convolution fusion | flops 79691776 | bytes 2393088 | tf_op jit(solution)/shard_map/while/body/eval_jaxpr/dot_general | solution.py:39
  123.1 1.7 convolution_add_fusion.5
  124.8 1.5 collective-permute-start
  126.3 3.2 %collective-permute-start.2 = (f32[256,128]{1,0:T(8,128)S(1)}, f32[256,128]{1,0:T(8,128)}, u32[]{:S(2)}, u32[]{:S(2)}) collective-permute-start(f32[256,128]{1,0:T(8,128)S(1)} %broadcast_select_fusion.2), channel_id=1, source_target_pairs={{0,16},{16,32},{32,48},{48,64},{64,80},{80,96},{96,112},{112,128},... | collective-permute-start | bytes 393224 | tf_op jit(solution)/shard_map/while/body/eval_jaxpr/ppermute | solution.py:15
  129.8 3.1 %multiply_convert_fusion.6 = bf16[4096,256]{1,0:T(8,128)(2,1)S(1)} fusion(bf16[4096,32]{1,0:T(8,128)(2,1)S(1)} %get-tuple-element.181, bf16[256,32]{1,0:T(8,128)(2,1)S(1)} %collective-permute-done, f32[256]{0:T(256)S(1)} %multiply_reduce_fusion.8, f32[4096]{0:T(1024)S(1)} %get-tuple-element.180), kind=kOutput, calls=%fused_computation.2.clone.1 | convolution fusion | flops 79691776 | bytes 2393088 | tf_op jit(solution)/shard_map/while/body/eval_jaxpr/dot_general | solution.py:39
  134.7 1.7 convolution_add_fusion.5
  136.4 1.5 collective-permute-start
  138.0 3.2 %collective-permute-start.2 = (f32[256,128]{1,0:T(8,128)S(1)}, f32[256,128]{1,0:T(8,128)}, u32[]{:S(2)}, u32[]{:S(2)}) collective-permute-start(f32[256,128]{1,0:T(8,128)S(1)} %broadcast_select_fusion.2), channel_id=1, source_target_pairs={{0,16},{16,32},{32,48},{48,64},{64,80},{80,96},{96,112},{112,128},... | collective-permute-start | bytes 393224 | tf_op jit(solution)/shard_map/while/body/eval_jaxpr/ppermute | solution.py:15
  141.4 3.1 %multiply_convert_fusion.6 = bf16[4096,256]{1,0:T(8,128)(2,1)S(1)} fusion(bf16[4096,32]{1,0:T(8,128)(2,1)S(1)} %get-tuple-element.181, bf16[256,32]{1,0:T(8,128)(2,1)S(1)} %collective-permute-done, f32[256]{0:T(256)S(1)} %multiply_reduce_fusion.8, f32[4096]{0:T(1024)S(1)} %get-tuple-element.180), kind=kOutput, calls=%fused_computation.2.clone.1 | convolution fusion | flops 79691776 | bytes 2393088 | tf_op jit(solution)/shard_map/while/body/eval_jaxpr/dot_general | solution.py:39
  146.4 1.7 convolution_add_fusion.5
  148.1 1.5 collective-permute-start
  149.6 3.2 %collective-permute-start.2 = (f32[256,128]{1,0:T(8,128)S(1)}, f32[256,128]{1,0:T(8,128)}, u32[]{:S(2)}, u32[]{:S(2)}) collective-permute-start(f32[256,128]{1,0:T(8,128)S(1)} %broadcast_select_fusion.2), channel_id=1, source_target_pairs={{0,16},{16,32},{32,48},{48,64},{64,80},{80,96},{96,112},{112,128},... | collective-permute-start | bytes 393224 | tf_op jit(solution)/shard_map/while/body/eval_jaxpr/ppermute | solution.py:15
  153.1 3.1 %multiply_convert_fusion.6 = bf16[4096,256]{1,0:T(8,128)(2,1)S(1)} fusion(bf16[4096,32]{1,0:T(8,128)(2,1)S(1)} %get-tuple-element.181, bf16[256,32]{1,0:T(8,128)(2,1)S(1)} %collective-permute-done, f32[256]{0:T(256)S(1)} %multiply_reduce_fusion.8, f32[4096]{0:T(1024)S(1)} %get-tuple-element.180), kind=kOutput, calls=%fused_computation.2.clone.1 | convolution fusion | flops 79691776 | bytes 2393088 | tf_op jit(solution)/shard_map/while/body/eval_jaxpr/dot_general | solution.py:39
  158.0 1.7 convolution_add_fusion.5
  159.7 1.5 collective-permute-start
  161.3 3.2 %collective-permute-start.2 = (f32[256,128]{1,0:T(8,128)S(1)}, f32[256,128]{1,0:T(8,128)}, u32[]{:S(2)}, u32[]{:S(2)}) collective-permute-start(f32[256,128]{1,0:T(8,128)S(1)} %broadcast_select_fusion.2), channel_id=1, source_target_pairs={{0,16},{16,32},{32,48},{48,64},{64,80},{80,96},{96,112},{112,128},... | collective-permute-start | bytes 393224 | tf_op jit(solution)/shard_map/while/body/eval_jaxpr/ppermute | solution.py:15
  164.7 3.1 %multiply_convert_fusion.6 = bf16[4096,256]{1,0:T(8,128)(2,1)S(1)} fusion(bf16[4096,32]{1,0:T(8,128)(2,1)S(1)} %get-tuple-element.181, bf16[256,32]{1,0:T(8,128)(2,1)S(1)} %collective-permute-done, f32[256]{0:T(256)S(1)} %multiply_reduce_fusion.8, f32[4096]{0:T(1024)S(1)} %get-tuple-element.180), kind=kOutput, calls=%fused_computation.2.clone.1 | convolution fusion | flops 79691776 | bytes 2393088 | tf_op jit(solution)/shard_map/while/body/eval_jaxpr/dot_general | solution.py:39
  169.7 1.7 convolution_add_fusion.5
  171.3 5.0 %fusion.4 = bf16[4096,128]{1,0:T(8,128)(2,1)} fusion(f32[4096,128]{1,0:T(8,128)S(1)} %get-tuple-element.46, bf16[256,128]{1,0:T(8,128)(2,1)} %copy-done.7, f32[256]{0:T(256)} %multiply_reduce_fusion.4, bf16[4096,32]{1,0:T(8,128)(2,1)S(1)} %get-tuple-element.189, bf16[256,32]{1,0:T(8,128)(2,1)} %copy-done.6, f32[4096]{0:T(1024)S(1)} %get-tuple-element.201), kind=kOutput, calls=%fused_computation.13 | convolution fusion | flops 349175808 | bytes 3507200 | tf_op jit(solution)/shard_map/dot_general | solution.py:78
  176.3 4.4 %all-to-all-start = ((bf16[16,256,128]{2,1,0:T(8,128)(2,1)}), bf16[16,256,128]{2,1,0:T(8,128)(2,1)S(1)}, u32[]{:S(2)}, u32[]{:S(2)}) async-start(bf16[16,256,128]{2,1,0:T(8,128)(2,1)} %bitcast.25), calls=%async_computation | async-start | bytes 2097152 | tf_op jit(solution)/shard_map/all_to_all | solution.py:25
  181.4 9.2 %collective-permute-start.5 = (f32[256,128]{1,0:T(8,128)S(1)}, f32[256,128]{1,0:T(8,128)S(1)}, u32[]{:S(2)}, u32[]{:S(2)}) collective-permute-start(f32[256,128]{1,0:T(8,128)S(1)} %get-tuple-element.47), channel_id=1, source_target_pairs={{0,144},{16,160},{32,176},{48,192},{64,208},{80,224},{96,240},{112... | collective-permute-start | bytes 393224 | tf_op jit(solution)/shard_map/ppermute | solution.py:15
  190.6 20.1 %all-to-all-done = bf16[16,256,128]{2,1,0:T(8,128)(2,1)S(1)} async-done(((bf16[16,256,128]{2,1,0:T(8,128)(2,1)}), bf16[16,256,128]{2,1,0:T(8,128)(2,1)S(1)}, u32[]{:S(2)}, u32[]{:S(2)}) %all-to-all-start) | async-done | bytes 1048608 | tf_op jit(solution)/shard_map/all_to_all | solution.py:25
  210.9 13.9 %all-reduce.1 = (f32[128]{0:T(128)S(1)}, f32[128]{0:T(128)S(1)}) all-reduce(f32[128]{0:T(128)S(1)} %multiply_reduce_fusion.6, f32[128]{0:T(128)S(1)} %multiply_reduce_fusion.3), channel_id=1, replica_groups=mesh['blk_0'=4,'blk_1'=2,'blk_2'=2,'wide_0'=2,'wide_1'=8] {'blk_0'}, use_global_device_ids=true, to_apply=%region_1.0 | all-reduce | flops 256 | bytes 2048 | tf_op jit(solution)/shard_map/psum | solution.py:30
  224.8 4.9 %all-reduce.4 = (f32[128]{0:T(128)S(1)}, f32[128]{0:T(128)S(1)}) all-reduce(f32[128]{0:T(128)S(1)} %get-tuple-element.93, f32[128]{0:T(128)S(1)} %get-tuple-element.94), channel_id=1, replica_groups=mesh['blk_0'=4,'blk_1'=2,'blk_2'=2,'wide_0'=2,'wide_1'=8] {'blk_1'}, use_global_device_ids=true, to_apply=%region_2.3 | all-reduce | flops 256 | bytes 2048 | tf_op jit(solution)/shard_map/psum | solution.py:30
  229.8 2.4 all-reduce.3
  232.2 6.4 %all-reduce.2 = (f32[128]{0:T(128)S(1)}, f32[128]{0:T(128)S(1)}) all-reduce(f32[128]{0:T(128)S(1)} %get-tuple-element.97, f32[128]{0:T(128)S(1)} %get-tuple-element.98), channel_id=1, replica_groups=mesh['blk_0'=4,'blk_1'=2,'blk_2'=2,'wide_0'=2,'wide_1'=8] {'wide_0'}, use_global_device_ids=true, to_apply=%region_4.0 | all-reduce | flops 256 | bytes 2048 | tf_op jit(solution)/shard_map/psum | solution.py:30
  238.6 15.1 %all-reduce = (f32[128]{0:T(128)S(1)}, f32[128]{0:T(128)S(1)}) all-reduce(f32[128]{0:T(128)S(1)} %get-tuple-element.95, f32[128]{0:T(128)S(1)} %get-tuple-element.96), channel_id=1, replica_groups=mesh['blk_0'=4,'blk_1'=2,'blk_2'=2,'wide_0'=2,'wide_1'=8] {'wide_1'}, use_global_device_ids=true, to_apply=%region_5.0 | all-reduce | flops 256 | bytes 2048 | tf_op jit(solution)/shard_map/psum | solution.py:30
  254.4 10.9 %psum.115 = f32[128]{0:T(128)S(1)} all-reduce(f32[128]{0:T(128)S(1)} %get-tuple-element.101), channel_id=1, replica_groups=mesh['blk_0'=4,'blk_1'=2,'blk_2'=2,'wide_0'=2,'wide_1'=8] {'blk_0'}, use_global_device_ids=true, to_apply=%region_20.0 | all-reduce | flops 128 | bytes 1024 | tf_op jit(solution)/shard_map/psum | solution.py:30
  265.4 4.9 %psum.116 = f32[128]{0:T(128)S(1)} all-reduce(f32[128]{0:T(128)S(1)} %psum.115), channel_id=1, replica_groups=mesh['blk_0'=4,'blk_1'=2,'blk_2'=2,'wide_0'=2,'wide_1'=8] {'blk_1'}, use_global_device_ids=true, to_apply=%region_21.0 | all-reduce | flops 128 | bytes 1024 | tf_op jit(solution)/shard_map/psum | solution.py:30
  270.3 2.4 psum.117
  272.7 6.4 %psum.118 = f32[128]{0:T(128)S(1)} all-reduce(f32[128]{0:T(128)S(1)} %psum.117), channel_id=1, replica_groups=mesh['blk_0'=4,'blk_1'=2,'blk_2'=2,'wide_0'=2,'wide_1'=8] {'wide_0'}, use_global_device_ids=true, to_apply=%region_23.0 | all-reduce | flops 128 | bytes 1024 | tf_op jit(solution)/shard_map/psum | solution.py:30
  279.2 15.2 %psum.119 = f32[128]{0:T(128)S(1)} all-reduce(f32[128]{0:T(128)S(1)} %psum.118), channel_id=1, replica_groups=mesh['blk_0'=4,'blk_1'=2,'blk_2'=2,'wide_0'=2,'wide_1'=8] {'wide_1'}, use_global_device_ids=true, to_apply=%region_24.0 | all-reduce | flops 128 | bytes 1024 | tf_op jit(solution)/shard_map/psum | solution.py:30
  (109 shorter events, 20.1 us)
Async XLA Ops:
  7.2 84.9 %all-gather.2.cloned.1.call-start = ((), (), s32[]{:S(2)}) async-start(), calls=%async_computation.1 | async-start | bytes 1114112 | tf_op jit(solution)/shard_map/all_gather | solution.py:53
  8.8 56.6 %copy-start.4 = (bf16[256,128]{1,0:T(8,128)(2,1)S(1)}, bf16[256,128]{1,0:T(8,128)(2,1)}, u32[]{:S(2)}) copy-start(bf16[256,128]{1,0:T(8,128)(2,1)} %convert_element_type.38) | copy-start | bytes 196612
  8.8 61.1 %collective-permute-start.4 = (bf16[256,128]{1,0:T(8,128)(2,1)}, bf16[256,128]{1,0:T(8,128)(2,1)S(1)}, u32[]{:S(2)}, u32[]{:S(2)}) collective-permute-start(bf16[256,128]{1,0:T(8,128)(2,1)} %convert_element_type.38), channel_id=1, source_target_pairs={{0,128},{16,144},{32,160},{48,176},{64,192},{80,208},{96,224},{112... | collective-permute-start | bytes 196616 | tf_op jit(solution)/shard_map/ppermute | solution.py:15
  13.1 56.0 %collective-permute-start.3 = (bf16[256,32]{1,0:T(8,128)(2,1)}, bf16[256,32]{1,0:T(8,128)(2,1)S(1)}, u32[]{:S(2)}, u32[]{:S(2)}) collective-permute-start(bf16[256,32]{1,0:T(8,128)(2,1)} %get-tuple-element.156), channel_id=1, source_target_pairs={{0,128},{16,144},{32,160},{48,176},{64,192},{80,208},{96,224},{112... | collective-permute-start | bytes 49160 | tf_op jit(solution)/shard_map/ppermute | solution.py:15
  69.2 22.9 %copy-start.6 = (bf16[256,32]{1,0:T(8,128)(2,1)}, bf16[256,32]{1,0:T(8,128)(2,1)S(1)}, u32[]{:S(2)}) copy-start(bf16[256,32]{1,0:T(8,128)(2,1)S(1)} %collective-permute-done.3) | copy-start | bytes 49156
  69.9 22.2 %copy-start.7 = (bf16[256,128]{1,0:T(8,128)(2,1)}, bf16[256,128]{1,0:T(8,128)(2,1)S(1)}, u32[]{:S(2)}) copy-start(bf16[256,128]{1,0:T(8,128)(2,1)S(1)} %collective-permute-done.4) | copy-start | bytes 196612
  92.1 3.9 %collective-permute-start = (bf16[256,32]{1,0:T(8,128)(2,1)}, bf16[256,32]{1,0:T(8,128)(2,1)S(1)}, u32[]{:S(2)}, u32[]{:S(2)}) collective-permute-start(bf16[256,32]{1,0:T(8,128)(2,1)} %get-tuple-element.166), channel_id=1, source_target_pairs={{0,16},{16,32},{32,48},{48,64},{64,80},{80,96},{96,112},{112,128},... | collective-permute-start | bytes 49160 | tf_op jit(solution)/shard_map/while/body/eval_jaxpr/ppermute | solution.py:15
  92.1 8.5 %collective-permute-start.2 = (f32[256,128]{1,0:T(8,128)S(1)}, f32[256,128]{1,0:T(8,128)}, u32[]{:S(2)}, u32[]{:S(2)}) collective-permute-start(f32[256,128]{1,0:T(8,128)S(1)} %broadcast_select_fusion.2), channel_id=1, source_target_pairs={{0,16},{16,32},{32,48},{48,64},{64,80},{80,96},{96,112},{112,128},... | collective-permute-start | bytes 393224 | tf_op jit(solution)/shard_map/while/body/eval_jaxpr/ppermute | solution.py:15
  94.6 5.2 %collective-permute-start.1 = (bf16[256,128]{1,0:T(8,128)(2,1)S(1)}, bf16[256,128]{1,0:T(8,128)(2,1)S(1)}, u32[]{:S(2)}, u32[]{:S(2)}) collective-permute-start(bf16[256,128]{1,0:T(8,128)(2,1)S(1)} %get-tuple-element.167), channel_id=1, source_target_pairs={{0,16},{16,32},{32,48},{48,64},{64,80},{80,96},{96,112},{112,128},... | collective-permute-start | bytes 196616 | tf_op jit(solution)/shard_map/while/body/eval_jaxpr/ppermute | solution.py:15
  99.8 1.2 copy-start
  102.7 4.0 %collective-permute-start = (bf16[256,32]{1,0:T(8,128)(2,1)}, bf16[256,32]{1,0:T(8,128)(2,1)S(1)}, u32[]{:S(2)}, u32[]{:S(2)}) collective-permute-start(bf16[256,32]{1,0:T(8,128)(2,1)} %get-tuple-element.166), channel_id=1, source_target_pairs={{0,16},{16,32},{32,48},{48,64},{64,80},{80,96},{96,112},{112,128},... | collective-permute-start | bytes 49160 | tf_op jit(solution)/shard_map/while/body/eval_jaxpr/ppermute | solution.py:15
  103.0 8.3 %collective-permute-start.2 = (f32[256,128]{1,0:T(8,128)S(1)}, f32[256,128]{1,0:T(8,128)}, u32[]{:S(2)}, u32[]{:S(2)}) collective-permute-start(f32[256,128]{1,0:T(8,128)S(1)} %broadcast_select_fusion.2), channel_id=1, source_target_pairs={{0,16},{16,32},{32,48},{48,64},{64,80},{80,96},{96,112},{112,128},... | collective-permute-start | bytes 393224 | tf_op jit(solution)/shard_map/while/body/eval_jaxpr/ppermute | solution.py:15
  106.3 4.3 %collective-permute-start.1 = (bf16[256,128]{1,0:T(8,128)(2,1)S(1)}, bf16[256,128]{1,0:T(8,128)(2,1)S(1)}, u32[]{:S(2)}, u32[]{:S(2)}) collective-permute-start(bf16[256,128]{1,0:T(8,128)(2,1)S(1)} %get-tuple-element.167), channel_id=1, source_target_pairs={{0,16},{16,32},{32,48},{48,64},{64,80},{80,96},{96,112},{112,128},... | collective-permute-start | bytes 196616 | tf_op jit(solution)/shard_map/while/body/eval_jaxpr/ppermute | solution.py:15
  110.6 1.2 copy-start
  113.5 4.5 %collective-permute-start = (bf16[256,32]{1,0:T(8,128)(2,1)}, bf16[256,32]{1,0:T(8,128)(2,1)S(1)}, u32[]{:S(2)}, u32[]{:S(2)}) collective-permute-start(bf16[256,32]{1,0:T(8,128)(2,1)} %get-tuple-element.166), channel_id=1, source_target_pairs={{0,16},{16,32},{32,48},{48,64},{64,80},{80,96},{96,112},{112,128},... | collective-permute-start | bytes 49160 | tf_op jit(solution)/shard_map/while/body/eval_jaxpr/ppermute | solution.py:15
  114.7 8.0 %collective-permute-start.2 = (f32[256,128]{1,0:T(8,128)S(1)}, f32[256,128]{1,0:T(8,128)}, u32[]{:S(2)}, u32[]{:S(2)}) collective-permute-start(f32[256,128]{1,0:T(8,128)S(1)} %broadcast_select_fusion.2), channel_id=1, source_target_pairs={{0,16},{16,32},{32,48},{48,64},{64,80},{80,96},{96,112},{112,128},... | collective-permute-start | bytes 393224 | tf_op jit(solution)/shard_map/while/body/eval_jaxpr/ppermute | solution.py:15
  117.9 3.9 %collective-permute-start.1 = (bf16[256,128]{1,0:T(8,128)(2,1)S(1)}, bf16[256,128]{1,0:T(8,128)(2,1)S(1)}, u32[]{:S(2)}, u32[]{:S(2)}) collective-permute-start(bf16[256,128]{1,0:T(8,128)(2,1)S(1)} %get-tuple-element.167), channel_id=1, source_target_pairs={{0,16},{16,32},{32,48},{48,64},{64,80},{80,96},{96,112},{112,128},... | collective-permute-start | bytes 196616 | tf_op jit(solution)/shard_map/while/body/eval_jaxpr/ppermute | solution.py:15
  121.9 1.2 copy-start
  124.8 4.9 %collective-permute-start = (bf16[256,32]{1,0:T(8,128)(2,1)}, bf16[256,32]{1,0:T(8,128)(2,1)S(1)}, u32[]{:S(2)}, u32[]{:S(2)}) collective-permute-start(bf16[256,32]{1,0:T(8,128)(2,1)} %get-tuple-element.166), channel_id=1, source_target_pairs={{0,16},{16,32},{32,48},{48,64},{64,80},{80,96},{96,112},{112,128},... | collective-permute-start | bytes 49160 | tf_op jit(solution)/shard_map/while/body/eval_jaxpr/ppermute | solution.py:15
  126.3 8.0 %collective-permute-start.2 = (f32[256,128]{1,0:T(8,128)S(1)}, f32[256,128]{1,0:T(8,128)}, u32[]{:S(2)}, u32[]{:S(2)}) collective-permute-start(f32[256,128]{1,0:T(8,128)S(1)} %broadcast_select_fusion.2), channel_id=1, source_target_pairs={{0,16},{16,32},{32,48},{48,64},{64,80},{80,96},{96,112},{112,128},... | collective-permute-start | bytes 393224 | tf_op jit(solution)/shard_map/while/body/eval_jaxpr/ppermute | solution.py:15
  129.6 3.9 %collective-permute-start.1 = (bf16[256,128]{1,0:T(8,128)(2,1)S(1)}, bf16[256,128]{1,0:T(8,128)(2,1)S(1)}, u32[]{:S(2)}, u32[]{:S(2)}) collective-permute-start(bf16[256,128]{1,0:T(8,128)(2,1)S(1)} %get-tuple-element.167), channel_id=1, source_target_pairs={{0,16},{16,32},{32,48},{48,64},{64,80},{80,96},{96,112},{112,128},... | collective-permute-start | bytes 196616 | tf_op jit(solution)/shard_map/while/body/eval_jaxpr/ppermute | solution.py:15
  133.5 1.2 copy-start
  136.4 4.9 %collective-permute-start = (bf16[256,32]{1,0:T(8,128)(2,1)}, bf16[256,32]{1,0:T(8,128)(2,1)S(1)}, u32[]{:S(2)}, u32[]{:S(2)}) collective-permute-start(bf16[256,32]{1,0:T(8,128)(2,1)} %get-tuple-element.166), channel_id=1, source_target_pairs={{0,16},{16,32},{32,48},{48,64},{64,80},{80,96},{96,112},{112,128},... | collective-permute-start | bytes 49160 | tf_op jit(solution)/shard_map/while/body/eval_jaxpr/ppermute | solution.py:15
  138.0 8.0 %collective-permute-start.2 = (f32[256,128]{1,0:T(8,128)S(1)}, f32[256,128]{1,0:T(8,128)}, u32[]{:S(2)}, u32[]{:S(2)}) collective-permute-start(f32[256,128]{1,0:T(8,128)S(1)} %broadcast_select_fusion.2), channel_id=1, source_target_pairs={{0,16},{16,32},{32,48},{48,64},{64,80},{80,96},{96,112},{112,128},... | collective-permute-start | bytes 393224 | tf_op jit(solution)/shard_map/while/body/eval_jaxpr/ppermute | solution.py:15
  141.2 3.9 %collective-permute-start.1 = (bf16[256,128]{1,0:T(8,128)(2,1)S(1)}, bf16[256,128]{1,0:T(8,128)(2,1)S(1)}, u32[]{:S(2)}, u32[]{:S(2)}) collective-permute-start(bf16[256,128]{1,0:T(8,128)(2,1)S(1)} %get-tuple-element.167), channel_id=1, source_target_pairs={{0,16},{16,32},{32,48},{48,64},{64,80},{80,96},{96,112},{112,128},... | collective-permute-start | bytes 196616 | tf_op jit(solution)/shard_map/while/body/eval_jaxpr/ppermute | solution.py:15
  145.1 1.2 copy-start
  148.1 4.9 %collective-permute-start = (bf16[256,32]{1,0:T(8,128)(2,1)}, bf16[256,32]{1,0:T(8,128)(2,1)S(1)}, u32[]{:S(2)}, u32[]{:S(2)}) collective-permute-start(bf16[256,32]{1,0:T(8,128)(2,1)} %get-tuple-element.166), channel_id=1, source_target_pairs={{0,16},{16,32},{32,48},{48,64},{64,80},{80,96},{96,112},{112,128},... | collective-permute-start | bytes 49160 | tf_op jit(solution)/shard_map/while/body/eval_jaxpr/ppermute | solution.py:15
  149.6 8.0 %collective-permute-start.2 = (f32[256,128]{1,0:T(8,128)S(1)}, f32[256,128]{1,0:T(8,128)}, u32[]{:S(2)}, u32[]{:S(2)}) collective-permute-start(f32[256,128]{1,0:T(8,128)S(1)} %broadcast_select_fusion.2), channel_id=1, source_target_pairs={{0,16},{16,32},{32,48},{48,64},{64,80},{80,96},{96,112},{112,128},... | collective-permute-start | bytes 393224 | tf_op jit(solution)/shard_map/while/body/eval_jaxpr/ppermute | solution.py:15
  152.8 3.9 %collective-permute-start.1 = (bf16[256,128]{1,0:T(8,128)(2,1)S(1)}, bf16[256,128]{1,0:T(8,128)(2,1)S(1)}, u32[]{:S(2)}, u32[]{:S(2)}) collective-permute-start(bf16[256,128]{1,0:T(8,128)(2,1)S(1)} %get-tuple-element.167), channel_id=1, source_target_pairs={{0,16},{16,32},{32,48},{48,64},{64,80},{80,96},{96,112},{112,128},... | collective-permute-start | bytes 196616 | tf_op jit(solution)/shard_map/while/body/eval_jaxpr/ppermute | solution.py:15
  156.8 1.2 copy-start
  159.7 4.9 %collective-permute-start = (bf16[256,32]{1,0:T(8,128)(2,1)}, bf16[256,32]{1,0:T(8,128)(2,1)S(1)}, u32[]{:S(2)}, u32[]{:S(2)}) collective-permute-start(bf16[256,32]{1,0:T(8,128)(2,1)} %get-tuple-element.166), channel_id=1, source_target_pairs={{0,16},{16,32},{32,48},{48,64},{64,80},{80,96},{96,112},{112,128},... | collective-permute-start | bytes 49160 | tf_op jit(solution)/shard_map/while/body/eval_jaxpr/ppermute | solution.py:15
  161.3 8.0 %collective-permute-start.2 = (f32[256,128]{1,0:T(8,128)S(1)}, f32[256,128]{1,0:T(8,128)}, u32[]{:S(2)}, u32[]{:S(2)}) collective-permute-start(f32[256,128]{1,0:T(8,128)S(1)} %broadcast_select_fusion.2), channel_id=1, source_target_pairs={{0,16},{16,32},{32,48},{48,64},{64,80},{80,96},{96,112},{112,128},... | collective-permute-start | bytes 393224 | tf_op jit(solution)/shard_map/while/body/eval_jaxpr/ppermute | solution.py:15
  164.5 3.9 %collective-permute-start.1 = (bf16[256,128]{1,0:T(8,128)(2,1)S(1)}, bf16[256,128]{1,0:T(8,128)(2,1)S(1)}, u32[]{:S(2)}, u32[]{:S(2)}) collective-permute-start(bf16[256,128]{1,0:T(8,128)(2,1)S(1)} %get-tuple-element.167), channel_id=1, source_target_pairs={{0,16},{16,32},{32,48},{48,64},{64,80},{80,96},{96,112},{112,128},... | collective-permute-start | bytes 196616 | tf_op jit(solution)/shard_map/while/body/eval_jaxpr/ppermute | solution.py:15
  168.4 1.2 copy-start
  176.3 5.0 %copy-start.2 = (f32[256,128]{1,0:T(8,128)S(1)}, f32[256,128]{1,0:T(8,128)}, u32[]{:S(2)}) copy-start(f32[256,128]{1,0:T(8,128)} %param.12) | copy-start | bytes 393220
  176.3 34.5 %copy-start.1 = (f32[256,128]{1,0:T(8,128)S(1)}, f32[256,128]{1,0:T(8,128)}, u32[]{:S(2)}) copy-start(f32[256,128]{1,0:T(8,128)} %param.13) | copy-start | bytes 393220
  176.3 77.4 %copy-start.5 = (f32[256,128]{1,0:T(8,128)S(1)}, f32[256,128]{1,0:T(8,128)}, u32[]{:S(2)}) copy-start(f32[256,128]{1,0:T(8,128)} %param.11) | copy-start | bytes 393220
  176.3 34.4 %all-to-all-start = ((bf16[16,256,128]{2,1,0:T(8,128)(2,1)}), bf16[16,256,128]{2,1,0:T(8,128)(2,1)S(1)}, u32[]{:S(2)}, u32[]{:S(2)}) async-start(bf16[16,256,128]{2,1,0:T(8,128)(2,1)} %bitcast.25), calls=%async_computation | async-start | bytes 2097152 | tf_op jit(solution)/shard_map/all_to_all | solution.py:25
  181.4 29.4 %collective-permute-start.5 = (f32[256,128]{1,0:T(8,128)S(1)}, f32[256,128]{1,0:T(8,128)S(1)}, u32[]{:S(2)}, u32[]{:S(2)}) collective-permute-start(f32[256,128]{1,0:T(8,128)S(1)} %get-tuple-element.47), channel_id=1, source_target_pairs={{0,144},{16,160},{32,176},{48,192},{64,208},{80,224},{96,240},{112... | collective-permute-start | bytes 393224 | tf_op jit(solution)/shard_map/ppermute | solution.py:15
  254.4 40.6 %copy-start.3 = (f32[256,128]{1,0:T(8,128)}, f32[256,128]{1,0:T(8,128)S(1)}, u32[]{:S(2)}) copy-start(f32[256,128]{1,0:T(8,128)S(1)} %get-tuple-element.102) | copy-start | bytes 393220
Sparse Core Ops, SparseCore 0:
  11.2 80.8 all-gather.1
where the time goes:
time: 303 us; the launch traced here: 302 us
  blocking collectives  133 us (44%)
  matrix products  47.5 us (16%)
  starting transfers between devices  47.4 us (16%)
  waiting for transfers between devices  43.9 us (14%)
  between operations  14.8 us (5%)
  local copies, waits for them, and re-layouts  8.25 us (3%)
  other arithmetic  6.69 us (2%)
    psum x10, blocking collectives, over_axes(): return functools.reduce(lax.psum, axes, x)  82.7 us
    all_gather x1, blocking collectives, on_device(): lax.all_gather(scaled, WIDE, axis=0, tiled=True)  50.2 us
    ppermute x24, starting transfers between devices, shifted(): return lax.ppermute(x, axis, [(i, (i + by) % count) for i in range(count)])  43 us
    all_gather x1, waiting for transfers between devices, on_device(): lax.all_gather(low_dir, WIDE, axis=0, tiled=True)  22.2 us
    dot_general x7, matrix products, kernel_tile(): lax.dot_general(rows_x, cols_x, (((1,), (1,)), ((), ())), preferred_eleme...  21.6 us
    all_to_all x1, waiting for transfers between devices, sent_and_summed(): blocks = lax.all_to_all(cut_along(x, dim, count), axis, 0, 0, tiled=True)  20.1 us
    dot_general x7, matrix products, paired_turn(): lax.dot_general(kernel_block, block_p, (((0,), (0,)), ((), ())), preferre...  11.7 us
    while x28, local copies, waits for them, and re-layouts  7.39 us
  transfers between devices with their start and end apart: 26, of which 4 were waited for; matrix products, arithmetic and copies ran while one was open for 13% of the time, Pallas kernels for 0%

commit v1 on v0

--- a/solution.py
+++ b/solution.py
@@ -4,10 +4,17 @@
 from jax import lax
 from jax.sharding import Mesh
 from jax.sharding import PartitionSpec as P
+from jax.lax import all_to_all, axis_size
 
 WIDE = ("wide_0", "wide_1")
 BLK = ("blk_0", "blk_1", "blk_2")
 BLK_WIDE = ("blk_0", "blk_1", "blk_2", "wide_0", "wide_1")
+
+
+def state_samples_all(mine_x, dim_k):
+    return jnp.concatenate(
+        all_to_all(jnp.stack(axis_size(WIDE) * [mine_x]), WIDE, 0, 0), axis=dim_k
+    )
 
 
 def shifted(x, axis, by):
@@ -50,7 +57,7 @@
     own_sq = squares_of(scaled)
     block_x, block_p = (
         lax.all_gather(scaled, WIDE, axis=0, tiled=True),
-        lax.all_gather(low_dir, WIDE, axis=0, tiled=True),
+        state_samples_all(low_dir, 0),
     )
     block_sq = squares_of(block_x)
     cycle_size = lax.axis_size(BLK)

time: 303 us -> 291 us (0.960)
  waiting for transfers between devices: 43.9 us -> 21.1 us
  between operations: 14.8 us -> 1.41 us
  blocking collectives: 133 us -> 143 us
  starting transfers between devices: 47.4 us -> 57.2 us
  matrix products: 47.5 us -> 55.4 us
    all_gather x1 -> x0, waiting for transfers between devices: 22.2 us -> none  [on_device(): lax.all_gather(low_dir, WIDE, axis=0, tiled=True)]
    all_to_all x0 -> x1, starting transfers between devices: none -> 10.3 us  [state_samples_all(): all_to_all(jnp.stack(axis_size(WIDE) * [mine_x]), WIDE, 0, 0)]
    all_gather x1, blocking collectives: 50.2 us -> 59.9 us  [on_device(): lax.all_gather(scaled, WIDE, axis=0, tiled=True)]
    dot_general x7, matrix products: 21.6 us -> 28.6 us  [kernel_tile(): lax.dot_general(rows_x, cols_x, (((1,), (1,)), ((), ())), preferred_eleme...]
    while x28 -> x14, local copies, waits for them, and re-layouts: 7.39 us -> 4.47 us
  transfers between devices with their start and end apart: 26 -> 26, of which waited for: 4 -> 3; matrix products, arithmetic and copies ran while one was open for 13% -> 16% of each run, Pallas kernels for 0% -> 0%
where the time goes in v1:
time: 291 us
  blocking collectives  143 us (49%)
  starting transfers between devices  57.2 us (20%)
  matrix products  55.4 us (19%)
  waiting for transfers between devices  21.1 us (7%)
  local copies, waits for them, and re-layouts  6.84 us (2%)
  other arithmetic  5.42 us (2%)
    psum x10, blocking collectives, over_axes(): return functools.reduce(lax.psum, axes, x)  82.8 us
    all_gather x1, blocking collectives, on_device(): lax.all_gather(scaled, WIDE, axis=0, tiled=True)  59.9 us
    ppermute x24, starting transfers between devices, shifted(): return lax.ppermute(x, axis, [(i, (i + by) % count) for i in range(count)])  43.1 us
    dot_general x7, matrix products, kernel_tile(): lax.dot_general(rows_x, cols_x, (((1,), (1,)), ((), ())), preferred_eleme...  28.6 us
    all_to_all x1, waiting for transfers between devices, sent_and_summed(): blocks = lax.all_to_all(cut_along(x, dim, count), axis, 0, 0, tiled=True)  19.3 us
    dot_general x7, matrix products, paired_turn(): lax.dot_general(kernel_block, block_p, (((0,), (0,)), ((), ())), preferre...  11.8 us
    all_to_all x1, starting transfers between devices, state_samples_all(): all_to_all(jnp.stack(axis_size(WIDE) * [mine_x]), WIDE, 0, 0)  10.3 us
  transfers between devices with their start and end apart: 26, of which 3 were waited for; matrix products, arithmetic and copies ran while one was open for 16% of the time, Pallas kernels for 0%

profile of v1, /device:TPU:10, one launch (start us, length us, event | category | flops | bytes accessed | tf_op | source)
XLA Modules:
  0.0 290.6 jit_solution(9810439706259020392)
XLA Ops:
  1.6 1.2 stack.2
  2.8 10.3 %all-to-all-start = ((bf16[16,256,128]{2,1,0:T(8,128)(2,1)}), bf16[16,256,128]{2,1,0:T(8,128)(2,1)S(1)}, u32[]{:S(2)}, u32[]{:S(2)}) async-start(bf16[16,256,128]{2,1,0:T(8,128)(2,1)} %stack.2), calls=%async_computation | async-start | bytes 2097152 | tf_op jit(solution)/shard_map/all_to_all | solution.py:16
  13.1 2.2 collective-permute-start.4
  16.1 1.4 collective-permute-start.3
  17.5 59.9 %all_gather.3 = bf16[4096,32]{1,0:T(8,128)(2,1)S(1)} all-gather(bf16[256,32]{1,0:T(8,128)(2,1)} %get-tuple-element.156), channel_id=1, replica_groups=mesh['blk_0'=4,'blk_1'=2,'blk_2'=2,'wide_0'=2,'wide_1'=8] {'wide_0','wid..., dimensions={0}, use_global_device_ids=true | all-gather | bytes 278528 | tf_op jit(solution)/shard_map/all_gather | solution.py:59
  78.5 4.2 %fusion.5 = f32[4096,128]{1,0:T(8,128)S(1)} fusion(bf16[256,128]{1,0:T(8,128)(2,1)S(1)} %convert_element_type.38, bf16[4096,32]{1,0:T(8,128)(2,1)} %copy-done, bf16[256,32]{1,0:T(8,128)(2,1)} %get-tuple-element.156, f32[256]{0:T(256)S(1)} %get-tuple-element.103, f32[4096]{0:T(1024)S(1)} %multiply_reduce_fusion.1), kind=kOutput, calls=%fused_computation.18 | convolution fusion | flops 348127232 | bytes 2458624 | tf_op jit(solution)/shard_map/dot_general | solution.py:66
  84.0 83.4 %while.17 = (s32[]{:T(128)}, bf16[256,32]{1,0:T(8,128)(2,1)}, bf16[256,128]{1,0:T(8,128)(2,1)S(1)}, f32[256,128]{1,0:T(8,128)S(1)}, f32[4096,128]{1,0:T(8,128)S(...) while((s32[]{:T(128)}, bf16[256,32]{1,0:T(8,128)(2,1)}, ...), condition=%wide.region_10.0_spmd.clone, body=%wide.region_8.10_spmd.clone.sunk | while | flops 617176832 | bytes 13453543 | solution.py:81
  84.0 2.5 collective-permute-start.2
  86.6 1.3 collective-permute-done
  88.0 4.1 %multiply_convert_fusion.6 = bf16[4096,256]{1,0:T(8,128)(2,1)S(1)} fusion(bf16[4096,32]{1,0:T(8,128)(2,1)} %get-tuple-element.181, bf16[256,32]{1,0:T(8,128)(2,1)S(1)} %collective-permute-done, f32[256]{0:T(256)S(1)} %multiply_reduce_fusion.8, f32[4096]{0:T(1024)S(1)} %get-tuple-element.180), kind=kOutput, calls=%fused_computation.2.clone.1 | convolution fusion | flops 79691776 | bytes 2393088 | tf_op jit(solution)/shard_map/while/body/eval_jaxpr/dot_general | solution.py:46
  93.6 1.7 convolution_add_fusion.5
  95.5 3.2 %collective-permute-start.2 = (f32[256,128]{1,0:T(8,128)S(1)}, f32[256,128]{1,0:T(8,128)}, u32[]{:S(2)}, u32[]{:S(2)}) collective-permute-start(f32[256,128]{1,0:T(8,128)S(1)} %broadcast_select_fusion.2), channel_id=1, source_target_pairs={{0,16},{16,32},{32,48},{48,64},{64,80},{80,96},{96,112},{112,128},... | collective-permute-start | bytes 393224 | tf_op jit(solution)/shard_map/while/body/eval_jaxpr/ppermute | solution.py:22
  99.4 4.1 %multiply_convert_fusion.6 = bf16[4096,256]{1,0:T(8,128)(2,1)S(1)} fusion(bf16[4096,32]{1,0:T(8,128)(2,1)} %get-tuple-element.181, bf16[256,32]{1,0:T(8,128)(2,1)S(1)} %collective-permute-done, f32[256]{0:T(256)S(1)} %multiply_reduce_fusion.8, f32[4096]{0:T(1024)S(1)} %get-tuple-element.180), kind=kOutput, calls=%fused_computation.2.clone.1 | convolution fusion | flops 79691776 | bytes 2393088 | tf_op jit(solution)/shard_map/while/body/eval_jaxpr/dot_general | solution.py:46
  104.9 1.7 convolution_add_fusion.5
  106.6 1.1 collective-permute-start
  107.8 3.2 %collective-permute-start.2 = (f32[256,128]{1,0:T(8,128)S(1)}, f32[256,128]{1,0:T(8,128)}, u32[]{:S(2)}, u32[]{:S(2)}) collective-permute-start(f32[256,128]{1,0:T(8,128)S(1)} %broadcast_select_fusion.2), channel_id=1, source_target_pairs={{0,16},{16,32},{32,48},{48,64},{64,80},{80,96},{96,112},{112,128},... | collective-permute-start | bytes 393224 | tf_op jit(solution)/shard_map/while/body/eval_jaxpr/ppermute | solution.py:22
  111.2 4.1 %multiply_convert_fusion.6 = bf16[4096,256]{1,0:T(8,128)(2,1)S(1)} fusion(bf16[4096,32]{1,0:T(8,128)(2,1)} %get-tuple-element.181, bf16[256,32]{1,0:T(8,128)(2,1)S(1)} %collective-permute-done, f32[256]{0:T(256)S(1)} %multiply_reduce_fusion.8, f32[4096]{0:T(1024)S(1)} %get-tuple-element.180), kind=kOutput, calls=%fused_computation.2.clone.1 | convolution fusion | flops 79691776 | bytes 2393088 | tf_op jit(solution)/shard_map/while/body/eval_jaxpr/dot_general | solution.py:46
  116.7 1.7 convolution_add_fusion.5
  118.4 1.5 collective-permute-start
  120.0 3.2 %collective-permute-start.2 = (f32[256,128]{1,0:T(8,128)S(1)}, f32[256,128]{1,0:T(8,128)}, u32[]{:S(2)}, u32[]{:S(2)}) collective-permute-start(f32[256,128]{1,0:T(8,128)S(1)} %broadcast_select_fusion.2), channel_id=1, source_target_pairs={{0,16},{16,32},{32,48},{48,64},{64,80},{80,96},{96,112},{112,128},... | collective-permute-start | bytes 393224 | tf_op jit(solution)/shard_map/while/body/eval_jaxpr/ppermute | solution.py:22
  123.4 4.1 %multiply_convert_fusion.6 = bf16[4096,256]{1,0:T(8,128)(2,1)S(1)} fusion(bf16[4096,32]{1,0:T(8,128)(2,1)} %get-tuple-element.181, bf16[256,32]{1,0:T(8,128)(2,1)S(1)} %collective-permute-done, f32[256]{0:T(256)S(1)} %multiply_reduce_fusion.8, f32[4096]{0:T(1024)S(1)} %get-tuple-element.180), kind=kOutput, calls=%fused_computation.2.clone.1 | convolution fusion | flops 79691776 | bytes 2393088 | tf_op jit(solution)/shard_map/while/body/eval_jaxpr/dot_general | solution.py:46
  129.0 1.7 convolution_add_fusion.5
  130.7 1.5 collective-permute-start
  132.2 3.2 %collective-permute-start.2 = (f32[256,128]{1,0:T(8,128)S(1)}, f32[256,128]{1,0:T(8,128)}, u32[]{:S(2)}, u32[]{:S(2)}) collective-permute-start(f32[256,128]{1,0:T(8,128)S(1)} %broadcast_select_fusion.2), channel_id=1, source_target_pairs={{0,16},{16,32},{32,48},{48,64},{64,80},{80,96},{96,112},{112,128},... | collective-permute-start | bytes 393224 | tf_op jit(solution)/shard_map/while/body/eval_jaxpr/ppermute | solution.py:22
  135.7 4.1 %multiply_convert_fusion.6 = bf16[4096,256]{1,0:T(8,128)(2,1)S(1)} fusion(bf16[4096,32]{1,0:T(8,128)(2,1)} %get-tuple-element.181, bf16[256,32]{1,0:T(8,128)(2,1)S(1)} %collective-permute-done, f32[256]{0:T(256)S(1)} %multiply_reduce_fusion.8, f32[4096]{0:T(1024)S(1)} %get-tuple-element.180), kind=kOutput, calls=%fused_computation.2.clone.1 | convolution fusion | flops 79691776 | bytes 2393088 | tf_op jit(solution)/shard_map/while/body/eval_jaxpr/dot_general | solution.py:46
  141.2 1.7 convolution_add_fusion.5
  142.9 1.5 collective-permute-start
  144.5 3.2 %collective-permute-start.2 = (f32[256,128]{1,0:T(8,128)S(1)}, f32[256,128]{1,0:T(8,128)}, u32[]{:S(2)}, u32[]{:S(2)}) collective-permute-start(f32[256,128]{1,0:T(8,128)S(1)} %broadcast_select_fusion.2), channel_id=1, source_target_pairs={{0,16},{16,32},{32,48},{48,64},{64,80},{80,96},{96,112},{112,128},... | collective-permute-start | bytes 393224 | tf_op jit(solution)/shard_map/while/body/eval_jaxpr/ppermute | solution.py:22
  147.9 4.1 %multiply_convert_fusion.6 = bf16[4096,256]{1,0:T(8,128)(2,1)S(1)} fusion(bf16[4096,32]{1,0:T(8,128)(2,1)} %get-tuple-element.181, bf16[256,32]{1,0:T(8,128)(2,1)S(1)} %collective-permute-done, f32[256]{0:T(256)S(1)} %multiply_reduce_fusion.8, f32[4096]{0:T(1024)S(1)} %get-tuple-element.180), kind=kOutput, calls=%fused_computation.2.clone.1 | convolution fusion | flops 79691776 | bytes 2393088 | tf_op jit(solution)/shard_map/while/body/eval_jaxpr/dot_general | solution.py:46
  153.4 1.7 convolution_add_fusion.5
  155.1 1.5 collective-permute-start
  156.7 3.2 %collective-permute-start.2 = (f32[256,128]{1,0:T(8,128)S(1)}, f32[256,128]{1,0:T(8,128)}, u32[]{:S(2)}, u32[]{:S(2)}) collective-permute-start(f32[256,128]{1,0:T(8,128)S(1)} %broadcast_select_fusion.2), channel_id=1, source_target_pairs={{0,16},{16,32},{32,48},{48,64},{64,80},{80,96},{96,112},{112,128},... | collective-permute-start | bytes 393224 | tf_op jit(solution)/shard_map/while/body/eval_jaxpr/ppermute | solution.py:22
  160.1 4.1 %multiply_convert_fusion.6 = bf16[4096,256]{1,0:T(8,128)(2,1)S(1)} fusion(bf16[4096,32]{1,0:T(8,128)(2,1)} %get-tuple-element.181, bf16[256,32]{1,0:T(8,128)(2,1)S(1)} %collective-permute-done, f32[256]{0:T(256)S(1)} %multiply_reduce_fusion.8, f32[4096]{0:T(1024)S(1)} %get-tuple-element.180), kind=kOutput, calls=%fused_computation.2.clone.1 | convolution fusion | flops 79691776 | bytes 2393088 | tf_op jit(solution)/shard_map/while/body/eval_jaxpr/dot_general | solution.py:46
  165.7 1.7 convolution_add_fusion.5
  167.4 5.4 %fusion.4 = bf16[4096,128]{1,0:T(8,128)(2,1)} fusion(f32[4096,128]{1,0:T(8,128)S(1)} %get-tuple-element.46, bf16[256,128]{1,0:T(8,128)(2,1)} %copy-done.8, f32[256]{0:T(256)} %multiply_reduce_fusion.4, bf16[4096,32]{1,0:T(8,128)(2,1)} %get-tuple-element.188, bf16[256,32]{1,0:T(8,128)(2,1)} %copy-done.5, f32[4096]{0:T(1024)S(1)} %get-tuple-element.198), kind=kOutput, calls=%fused_computation.13 | convolution fusion | flops 349175808 | bytes 3507200 | tf_op jit(solution)/shard_map/dot_general | solution.py:85
  172.8 3.8 %all-to-all-start.1 = ((bf16[16,256,128]{2,1,0:T(8,128)(2,1)}), bf16[16,256,128]{2,1,0:T(8,128)(2,1)S(1)}, u32[]{:S(2)}, u32[]{:S(2)}) async-start(bf16[16,256,128]{2,1,0:T(8,128)(2,1)} %bitcast.27), calls=%async_computation.1 | async-start | bytes 2097152 | tf_op jit(solution)/shard_map/all_to_all | solution.py:32
  177.3 9.5 %collective-permute-start.5 = (f32[256,128]{1,0:T(8,128)S(1)}, f32[256,128]{1,0:T(8,128)S(1)}, u32[]{:S(2)}, u32[]{:S(2)}) collective-permute-start(f32[256,128]{1,0:T(8,128)S(1)} %get-tuple-element.47), channel_id=1, source_target_pairs={{0,144},{16,160},{32,176},{48,192},{64,208},{80,224},{96,240},{112... | collective-permute-start | bytes 393224 | tf_op jit(solution)/shard_map/ppermute | solution.py:22
  186.8 19.3 %all-to-all-done.1 = bf16[16,256,128]{2,1,0:T(8,128)(2,1)S(1)} async-done(((bf16[16,256,128]{2,1,0:T(8,128)(2,1)}), bf16[16,256,128]{2,1,0:T(8,128)(2,1)S(1)}, u32[]{:S(2)}, u32[]{:S(2)}) %all-to-all-start.1) | async-done | bytes 1048608 | tf_op jit(solution)/shard_map/all_to_all | solution.py:32
  206.3 14.0 %all-reduce.1 = (f32[128]{0:T(128)S(1)}, f32[128]{0:T(128)S(1)}) all-reduce(f32[128]{0:T(128)S(1)} %multiply_reduce_fusion.6, f32[128]{0:T(128)S(1)} %multiply_reduce_fusion.3), channel_id=1, replica_groups=mesh['blk_0'=4,'blk_1'=2,'blk_2'=2,'wide_0'=2,'wide_1'=8] {'blk_0'}, use_global_device_ids=true, to_apply=%region_1.0 | all-reduce | flops 256 | bytes 2048 | tf_op jit(solution)/shard_map/psum | solution.py:37
  220.4 4.9 %all-reduce.4 = (f32[128]{0:T(128)S(1)}, f32[128]{0:T(128)S(1)}) all-reduce(f32[128]{0:T(128)S(1)} %get-tuple-element.93, f32[128]{0:T(128)S(1)} %get-tuple-element.94), channel_id=1, replica_groups=mesh['blk_0'=4,'blk_1'=2,'blk_2'=2,'wide_0'=2,'wide_1'=8] {'blk_1'}, use_global_device_ids=true, to_apply=%region_2.3 | all-reduce | flops 256 | bytes 2048 | tf_op jit(solution)/shard_map/psum | solution.py:37
  225.3 2.4 all-reduce.3
  227.7 6.4 %all-reduce.2 = (f32[128]{0:T(128)S(1)}, f32[128]{0:T(128)S(1)}) all-reduce(f32[128]{0:T(128)S(1)} %get-tuple-element.97, f32[128]{0:T(128)S(1)} %get-tuple-element.98), channel_id=1, replica_groups=mesh['blk_0'=4,'blk_1'=2,'blk_2'=2,'wide_0'=2,'wide_1'=8] {'wide_0'}, use_global_device_ids=true, to_apply=%region_4.0 | all-reduce | flops 256 | bytes 2048 | tf_op jit(solution)/shard_map/psum | solution.py:37
  234.2 15.1 %all-reduce = (f32[128]{0:T(128)S(1)}, f32[128]{0:T(128)S(1)}) all-reduce(f32[128]{0:T(128)S(1)} %get-tuple-element.95, f32[128]{0:T(128)S(1)} %get-tuple-element.96), channel_id=1, replica_groups=mesh['blk_0'=4,'blk_1'=2,'blk_2'=2,'wide_0'=2,'wide_1'=8] {'wide_1'}, use_global_device_ids=true, to_apply=%region_5.0 | all-reduce | flops 256 | bytes 2048 | tf_op jit(solution)/shard_map/psum | solution.py:37
  250.0 10.9 %psum.115 = f32[128]{0:T(128)S(1)} all-reduce(f32[128]{0:T(128)S(1)} %get-tuple-element.101), channel_id=1, replica_groups=mesh['blk_0'=4,'blk_1'=2,'blk_2'=2,'wide_0'=2,'wide_1'=8] {'blk_0'}, use_global_device_ids=true, to_apply=%region_20.0 | all-reduce | flops 128 | bytes 1024 | tf_op jit(solution)/shard_map/psum | solution.py:37
  260.9 4.9 %psum.116 = f32[128]{0:T(128)S(1)} all-reduce(f32[128]{0:T(128)S(1)} %psum.115), channel_id=1, replica_groups=mesh['blk_0'=4,'blk_1'=2,'blk_2'=2,'wide_0'=2,'wide_1'=8] {'blk_1'}, use_global_device_ids=true, to_apply=%region_21.0 | all-reduce | flops 128 | bytes 1024 | tf_op jit(solution)/shard_map/psum | solution.py:37
  265.8 2.4 psum.117
  268.3 6.4 %psum.118 = f32[128]{0:T(128)S(1)} all-reduce(f32[128]{0:T(128)S(1)} %psum.117), channel_id=1, replica_groups=mesh['blk_0'=4,'blk_1'=2,'blk_2'=2,'wide_0'=2,'wide_1'=8] {'wide_0'}, use_global_device_ids=true, to_apply=%region_23.0 | all-reduce | flops 128 | bytes 1024 | tf_op jit(solution)/shard_map/psum | solution.py:37
  274.7 15.2 %psum.119 = f32[128]{0:T(128)S(1)} all-reduce(f32[128]{0:T(128)S(1)} %psum.118), channel_id=1, replica_groups=mesh['blk_0'=4,'blk_1'=2,'blk_2'=2,'wide_0'=2,'wide_1'=8] {'wide_1'}, use_global_device_ids=true, to_apply=%region_24.0 | all-reduce | flops 128 | bytes 1024 | tf_op jit(solution)/shard_map/psum | solution.py:37
  (99 shorter events, 17.8 us)
Async XLA Ops:
  0.6 14.7 %copy-start.6 = (bf16[256,32]{0,1:T(8,128)(2,1)S(1)}, bf16[256,32]{0,1:T(8,128)(2,1)}, u32[]{:S(2)}) copy-start(bf16[256,32]{0,1:T(8,128)(2,1)} %param.8) | copy-start | bytes 49156
  0.6 14.8 %copy-start.7 = (f32[32]{0:T(128)S(1)}, f32[32]{0:T(128)}, u32[]{:S(2)}) copy-start(f32[32]{0:T(128)} %param.9) | copy-start | bytes 388
  2.8 80.6 %all-to-all-start = ((bf16[16,256,128]{2,1,0:T(8,128)(2,1)}), bf16[16,256,128]{2,1,0:T(8,128)(2,1)S(1)}, u32[]{:S(2)}, u32[]{:S(2)}) async-start(bf16[16,256,128]{2,1,0:T(8,128)(2,1)} %stack.2), calls=%async_computation | async-start | bytes 2097152 | tf_op jit(solution)/shard_map/all_to_all | solution.py:16
  13.1 70.3 %collective-permute-start.4 = (bf16[256,128]{1,0:T(8,128)(2,1)S(1)}, bf16[256,128]{1,0:T(8,128)(2,1)S(1)}, u32[]{:S(2)}, u32[]{:S(2)}) collective-permute-start(bf16[256,128]{1,0:T(8,128)(2,1)S(1)} %convert_element_type.38), channel_id=1, source_target_pairs={{0,128},{16,144},{32,160},{48,176},{64,192},{80,208},{96,224},{112... | collective-permute-start | bytes 196616 | tf_op jit(solution)/shard_map/ppermute | solution.py:22
  16.1 66.5 %collective-permute-start.3 = (bf16[256,32]{1,0:T(8,128)(2,1)}, bf16[256,32]{1,0:T(8,128)(2,1)S(1)}, u32[]{:S(2)}, u32[]{:S(2)}) collective-permute-start(bf16[256,32]{1,0:T(8,128)(2,1)} %get-tuple-element.156), channel_id=1, source_target_pairs={{0,128},{16,144},{32,160},{48,176},{64,192},{80,208},{96,224},{112... | collective-permute-start | bytes 49160 | tf_op jit(solution)/shard_map/ppermute | solution.py:22
  77.5 1.0 copy-start
  82.7 0.7 copy-start.5
  83.4 0.6 copy-start.8
  84.0 3.9 %collective-permute-start = (bf16[256,32]{1,0:T(8,128)(2,1)}, bf16[256,32]{1,0:T(8,128)(2,1)S(1)}, u32[]{:S(2)}, u32[]{:S(2)}) collective-permute-start(bf16[256,32]{1,0:T(8,128)(2,1)} %get-tuple-element.166), channel_id=1, source_target_pairs={{0,16},{16,32},{32,48},{48,64},{64,80},{80,96},{96,112},{112,128},... | collective-permute-start | bytes 49160 | tf_op jit(solution)/shard_map/while/body/eval_jaxpr/ppermute | solution.py:22
  84.0 9.5 %collective-permute-start.2 = (f32[256,128]{1,0:T(8,128)S(1)}, f32[256,128]{1,0:T(8,128)}, u32[]{:S(2)}, u32[]{:S(2)}) collective-permute-start(f32[256,128]{1,0:T(8,128)S(1)} %broadcast_select_fusion.2), channel_id=1, source_target_pairs={{0,16},{16,32},{32,48},{48,64},{64,80},{80,96},{96,112},{112,128},... | collective-permute-start | bytes 393224 | tf_op jit(solution)/shard_map/while/body/eval_jaxpr/ppermute | solution.py:22
  86.5 6.3 %collective-permute-start.1 = (bf16[256,128]{1,0:T(8,128)(2,1)S(1)}, bf16[256,128]{1,0:T(8,128)(2,1)S(1)}, u32[]{:S(2)}, u32[]{:S(2)}) collective-permute-start(bf16[256,128]{1,0:T(8,128)(2,1)S(1)} %get-tuple-element.167), channel_id=1, source_target_pairs={{0,16},{16,32},{32,48},{48,64},{64,80},{80,96},{96,112},{112,128},... | collective-permute-start | bytes 196616 | tf_op jit(solution)/shard_map/while/body/eval_jaxpr/ppermute | solution.py:22
  95.3 4.0 %collective-permute-start = (bf16[256,32]{1,0:T(8,128)(2,1)}, bf16[256,32]{1,0:T(8,128)(2,1)S(1)}, u32[]{:S(2)}, u32[]{:S(2)}) collective-permute-start(bf16[256,32]{1,0:T(8,128)(2,1)} %get-tuple-element.166), channel_id=1, source_target_pairs={{0,16},{16,32},{32,48},{48,64},{64,80},{80,96},{96,112},{112,128},... | collective-permute-start | bytes 49160 | tf_op jit(solution)/shard_map/while/body/eval_jaxpr/ppermute | solution.py:22
  95.5 9.4 %collective-permute-start.2 = (f32[256,128]{1,0:T(8,128)S(1)}, f32[256,128]{1,0:T(8,128)}, u32[]{:S(2)}, u32[]{:S(2)}) collective-permute-start(f32[256,128]{1,0:T(8,128)S(1)} %broadcast_select_fusion.2), channel_id=1, source_target_pairs={{0,16},{16,32},{32,48},{48,64},{64,80},{80,96},{96,112},{112,128},... | collective-permute-start | bytes 393224 | tf_op jit(solution)/shard_map/while/body/eval_jaxpr/ppermute | solution.py:22
  98.7 5.4 %collective-permute-start.1 = (bf16[256,128]{1,0:T(8,128)(2,1)S(1)}, bf16[256,128]{1,0:T(8,128)(2,1)S(1)}, u32[]{:S(2)}, u32[]{:S(2)}) collective-permute-start(bf16[256,128]{1,0:T(8,128)(2,1)S(1)} %get-tuple-element.167), channel_id=1, source_target_pairs={{0,16},{16,32},{32,48},{48,64},{64,80},{80,96},{96,112},{112,128},... | collective-permute-start | bytes 196616 | tf_op jit(solution)/shard_map/while/body/eval_jaxpr/ppermute | solution.py:22
  106.6 4.4 %collective-permute-start = (bf16[256,32]{1,0:T(8,128)(2,1)}, bf16[256,32]{1,0:T(8,128)(2,1)S(1)}, u32[]{:S(2)}, u32[]{:S(2)}) collective-permute-start(bf16[256,32]{1,0:T(8,128)(2,1)} %get-tuple-element.166), channel_id=1, source_target_pairs={{0,16},{16,32},{32,48},{48,64},{64,80},{80,96},{96,112},{112,128},... | collective-permute-start | bytes 49160 | tf_op jit(solution)/shard_map/while/body/eval_jaxpr/ppermute | solution.py:22
  107.8 9.0 %collective-permute-start.2 = (f32[256,128]{1,0:T(8,128)S(1)}, f32[256,128]{1,0:T(8,128)}, u32[]{:S(2)}, u32[]{:S(2)}) collective-permute-start(f32[256,128]{1,0:T(8,128)S(1)} %broadcast_select_fusion.2), channel_id=1, source_target_pairs={{0,16},{16,32},{32,48},{48,64},{64,80},{80,96},{96,112},{112,128},... | collective-permute-start | bytes 393224 | tf_op jit(solution)/shard_map/while/body/eval_jaxpr/ppermute | solution.py:22
  111.0 4.9 %collective-permute-start.1 = (bf16[256,128]{1,0:T(8,128)(2,1)S(1)}, bf16[256,128]{1,0:T(8,128)(2,1)S(1)}, u32[]{:S(2)}, u32[]{:S(2)}) collective-permute-start(bf16[256,128]{1,0:T(8,128)(2,1)S(1)} %get-tuple-element.167), channel_id=1, source_target_pairs={{0,16},{16,32},{32,48},{48,64},{64,80},{80,96},{96,112},{112,128},... | collective-permute-start | bytes 196616 | tf_op jit(solution)/shard_map/while/body/eval_jaxpr/ppermute | solution.py:22
  118.4 4.9 %collective-permute-start = (bf16[256,32]{1,0:T(8,128)(2,1)}, bf16[256,32]{1,0:T(8,128)(2,1)S(1)}, u32[]{:S(2)}, u32[]{:S(2)}) collective-permute-start(bf16[256,32]{1,0:T(8,128)(2,1)} %get-tuple-element.166), channel_id=1, source_target_pairs={{0,16},{16,32},{32,48},{48,64},{64,80},{80,96},{96,112},{112,128},... | collective-permute-start | bytes 49160 | tf_op jit(solution)/shard_map/while/body/eval_jaxpr/ppermute | solution.py:22
  120.0 9.0 %collective-permute-start.2 = (f32[256,128]{1,0:T(8,128)S(1)}, f32[256,128]{1,0:T(8,128)}, u32[]{:S(2)}, u32[]{:S(2)}) collective-permute-start(f32[256,128]{1,0:T(8,128)S(1)} %broadcast_select_fusion.2), channel_id=1, source_target_pairs={{0,16},{16,32},{32,48},{48,64},{64,80},{80,96},{96,112},{112,128},... | collective-permute-start | bytes 393224 | tf_op jit(solution)/shard_map/while/body/eval_jaxpr/ppermute | solution.py:22
  123.2 4.9 %collective-permute-start.1 = (bf16[256,128]{1,0:T(8,128)(2,1)S(1)}, bf16[256,128]{1,0:T(8,128)(2,1)S(1)}, u32[]{:S(2)}, u32[]{:S(2)}) collective-permute-start(bf16[256,128]{1,0:T(8,128)(2,1)S(1)} %get-tuple-element.167), channel_id=1, source_target_pairs={{0,16},{16,32},{32,48},{48,64},{64,80},{80,96},{96,112},{112,128},... | collective-permute-start | bytes 196616 | tf_op jit(solution)/shard_map/while/body/eval_jaxpr/ppermute | solution.py:22
  130.7 4.9 %collective-permute-start = (bf16[256,32]{1,0:T(8,128)(2,1)}, bf16[256,32]{1,0:T(8,128)(2,1)S(1)}, u32[]{:S(2)}, u32[]{:S(2)}) collective-permute-start(bf16[256,32]{1,0:T(8,128)(2,1)} %get-tuple-element.166), channel_id=1, source_target_pairs={{0,16},{16,32},{32,48},{48,64},{64,80},{80,96},{96,112},{112,128},... | collective-permute-start | bytes 49160 | tf_op jit(solution)/shard_map/while/body/eval_jaxpr/ppermute | solution.py:22
  132.2 9.0 %collective-permute-start.2 = (f32[256,128]{1,0:T(8,128)S(1)}, f32[256,128]{1,0:T(8,128)}, u32[]{:S(2)}, u32[]{:S(2)}) collective-permute-start(f32[256,128]{1,0:T(8,128)S(1)} %broadcast_select_fusion.2), channel_id=1, source_target_pairs={{0,16},{16,32},{32,48},{48,64},{64,80},{80,96},{96,112},{112,128},... | collective-permute-start | bytes 393224 | tf_op jit(solution)/shard_map/while/body/eval_jaxpr/ppermute | solution.py:22
  135.5 4.9 %collective-permute-start.1 = (bf16[256,128]{1,0:T(8,128)(2,1)S(1)}, bf16[256,128]{1,0:T(8,128)(2,1)S(1)}, u32[]{:S(2)}, u32[]{:S(2)}) collective-permute-start(bf16[256,128]{1,0:T(8,128)(2,1)S(1)} %get-tuple-element.167), channel_id=1, source_target_pairs={{0,16},{16,32},{32,48},{48,64},{64,80},{80,96},{96,112},{112,128},... | collective-permute-start | bytes 196616 | tf_op jit(solution)/shard_map/while/body/eval_jaxpr/ppermute | solution.py:22
  142.9 4.9 %collective-permute-start = (bf16[256,32]{1,0:T(8,128)(2,1)}, bf16[256,32]{1,0:T(8,128)(2,1)S(1)}, u32[]{:S(2)}, u32[]{:S(2)}) collective-permute-start(bf16[256,32]{1,0:T(8,128)(2,1)} %get-tuple-element.166), channel_id=1, source_target_pairs={{0,16},{16,32},{32,48},{48,64},{64,80},{80,96},{96,112},{112,128},... | collective-permute-start | bytes 49160 | tf_op jit(solution)/shard_map/while/body/eval_jaxpr/ppermute | solution.py:22
  144.5 9.0 %collective-permute-start.2 = (f32[256,128]{1,0:T(8,128)S(1)}, f32[256,128]{1,0:T(8,128)}, u32[]{:S(2)}, u32[]{:S(2)}) collective-permute-start(f32[256,128]{1,0:T(8,128)S(1)} %broadcast_select_fusion.2), channel_id=1, source_target_pairs={{0,16},{16,32},{32,48},{48,64},{64,80},{80,96},{96,112},{112,128},... | collective-permute-start | bytes 393224 | tf_op jit(solution)/shard_map/while/body/eval_jaxpr/ppermute | solution.py:22
  147.7 4.9 %collective-permute-start.1 = (bf16[256,128]{1,0:T(8,128)(2,1)S(1)}, bf16[256,128]{1,0:T(8,128)(2,1)S(1)}, u32[]{:S(2)}, u32[]{:S(2)}) collective-permute-start(bf16[256,128]{1,0:T(8,128)(2,1)S(1)} %get-tuple-element.167), channel_id=1, source_target_pairs={{0,16},{16,32},{32,48},{48,64},{64,80},{80,96},{96,112},{112,128},... | collective-permute-start | bytes 196616 | tf_op jit(solution)/shard_map/while/body/eval_jaxpr/ppermute | solution.py:22
  155.1 4.9 %collective-permute-start = (bf16[256,32]{1,0:T(8,128)(2,1)}, bf16[256,32]{1,0:T(8,128)(2,1)S(1)}, u32[]{:S(2)}, u32[]{:S(2)}) collective-permute-start(bf16[256,32]{1,0:T(8,128)(2,1)} %get-tuple-element.166), channel_id=1, source_target_pairs={{0,16},{16,32},{32,48},{48,64},{64,80},{80,96},{96,112},{112,128},... | collective-permute-start | bytes 49160 | tf_op jit(solution)/shard_map/while/body/eval_jaxpr/ppermute | solution.py:22
  156.7 9.0 %collective-permute-start.2 = (f32[256,128]{1,0:T(8,128)S(1)}, f32[256,128]{1,0:T(8,128)}, u32[]{:S(2)}, u32[]{:S(2)}) collective-permute-start(f32[256,128]{1,0:T(8,128)S(1)} %broadcast_select_fusion.2), channel_id=1, source_target_pairs={{0,16},{16,32},{32,48},{48,64},{64,80},{80,96},{96,112},{112,128},... | collective-permute-start | bytes 393224 | tf_op jit(solution)/shard_map/while/body/eval_jaxpr/ppermute | solution.py:22
  159.9 4.9 %collective-permute-start.1 = (bf16[256,128]{1,0:T(8,128)(2,1)S(1)}, bf16[256,128]{1,0:T(8,128)(2,1)S(1)}, u32[]{:S(2)}, u32[]{:S(2)}) collective-permute-start(bf16[256,128]{1,0:T(8,128)(2,1)S(1)} %get-tuple-element.167), channel_id=1, source_target_pairs={{0,16},{16,32},{32,48},{48,64},{64,80},{80,96},{96,112},{112,128},... | collective-permute-start | bytes 196616 | tf_op jit(solution)/shard_map/while/body/eval_jaxpr/ppermute | solution.py:22
  172.8 4.5 %copy-start.2 = (f32[256,128]{1,0:T(8,128)S(1)}, f32[256,128]{1,0:T(8,128)}, u32[]{:S(2)}) copy-start(f32[256,128]{1,0:T(8,128)} %param.12) | copy-start | bytes 393220
  172.8 33.5 %copy-start.1 = (f32[256,128]{1,0:T(8,128)S(1)}, f32[256,128]{1,0:T(8,128)}, u32[]{:S(2)}) copy-start(f32[256,128]{1,0:T(8,128)} %param.13) | copy-start | bytes 393220
  172.8 76.5 %copy-start.4 = (f32[256,128]{1,0:T(8,128)S(1)}, f32[256,128]{1,0:T(8,128)}, u32[]{:S(2)}) copy-start(f32[256,128]{1,0:T(8,128)} %param.11) | copy-start | bytes 393220
  172.8 33.3 %all-to-all-start.1 = ((bf16[16,256,128]{2,1,0:T(8,128)(2,1)}), bf16[16,256,128]{2,1,0:T(8,128)(2,1)S(1)}, u32[]{:S(2)}, u32[]{:S(2)}) async-start(bf16[16,256,128]{2,1,0:T(8,128)(2,1)} %bitcast.27), calls=%async_computation.1 | async-start | bytes 2097152 | tf_op jit(solution)/shard_map/all_to_all | solution.py:32
  177.3 29.0 %collective-permute-start.5 = (f32[256,128]{1,0:T(8,128)S(1)}, f32[256,128]{1,0:T(8,128)S(1)}, u32[]{:S(2)}, u32[]{:S(2)}) collective-permute-start(f32[256,128]{1,0:T(8,128)S(1)} %get-tuple-element.47), channel_id=1, source_target_pairs={{0,144},{16,160},{32,176},{48,192},{64,208},{80,224},{96,240},{112... | collective-permute-start | bytes 393224 | tf_op jit(solution)/shard_map/ppermute | solution.py:22
  250.0 40.6 %copy-start.3 = (f32[256,128]{1,0:T(8,128)}, f32[256,128]{1,0:T(8,128)S(1)}, u32[]{:S(2)}) copy-start(f32[256,128]{1,0:T(8,128)S(1)} %get-tuple-element.102) | copy-start | bytes 393220
